TPU v7x, 128 devices: a whole 4x4x4 slice. The times are simulated.
128 devices in a mesh: group: 8 (over z, core), block: 16 (over y, x).
Axes of the slice: x: 4, y: 4, z: 4, core: 2. Of those that a mesh axis runs over, the one named last changes fastest.
Arguments:
- embeddings: float32 [65536, 1024], P(('group', 'block')), may hold values from -6 to 6
- labels: int32 [65536, 1], P(('group', 'block')), may hold values from 0 to 7; in each aligned block of 512 rows (0 to 511, 512 to 1023, ...) at most 96 rows name the same one
- row_ids: int32 [65536], P(('group', 'block')), may hold values from 0 to 65535, each once
Outputs:
- dup_score: float32 [65536], P(('group', 'block'))
Inputs may be any that keep to these rules, and one draw needn't show every extreme that they name: `labels`: among the rows of one device (aligned blocks of 512 rows) no cluster appears more than 96 times; some cluster appears exactly 96 times. `row_ids`: every value appears exactly once.
All inputs are finite; a program needn't handle non-finite values.
Results may differ from a plain program's by a relative error of at most 0.0012.
Values may be sent and summed in bfloat16 or wider, within the bound.
No kernel may reach another device: no remote copies, remote signals or barrier semaphores. Data moves between devices by JAX's collectives and lax.ppermute only.
A program may use at most 128 MiB of HBM per device.

v0:
```python
import jax
import jax.numpy as jnp
from jax import lax
from jax.sharding import PartitionSpec as P


def per_device(embeddings, labels, row_ids):
    groups = lax.axis_size("group")
    row_count = embeddings.shape[0]
    features = embeddings.shape[1]
    capacity = row_count * 3 // (2 * groups)
    scale = lax.rsqrt(jnp.sum(embeddings * embeddings, axis=1, keepdims=True) + 1e-06)
    normed = (embeddings * scale).astype(jnp.bfloat16)
    row_labels = labels[:, 0]
    onehot = (row_labels[:, None] == jnp.arange(groups, dtype=jnp.int32)[None, :]).astype(jnp.int32)
    ranks = jnp.sum((jnp.cumsum(onehot, axis=0) - 1) * onehot, axis=1)
    slot_index = row_labels * capacity + ranks
    send_rows = jnp.zeros((groups * capacity, features), jnp.bfloat16).at[slot_index].set(normed)
    send_ids = jnp.full((groups * capacity,), -1, jnp.int32).at[slot_index].set(row_ids)
    local_rows, local_ids = (
        lax.all_to_all(send_rows, "group", split_axis=0, concat_axis=0, tiled=True),
        lax.all_to_all(send_ids, "group", split_axis=0, concat_axis=0, tiled=True),
    )
    initial = jnp.full((local_rows.shape[0],), -1.0, jnp.float32)
    peer_ids = lax.all_gather(local_ids, "block", axis=0, tiled=True)
    scores = jnp.dot(
        local_rows,
        lax.all_gather(local_rows, "block", axis=0, tiled=True).T,
        preferred_element_type=jnp.float32,
    )
    earlier = (peer_ids[None, :] >= 0) & (peer_ids[None, :] < local_ids[:, None])
    running = (jnp.maximum(initial, jnp.max(jnp.where(earlier, scores, -1.0), axis=1)), scores)[0]
    returned_max = lax.all_to_all(running, "group", split_axis=0, concat_axis=0, tiled=True)
    return returned_max[slot_index]


def solution(mesh):
    placed = (P(("group", "block"), None), P(("group", "block"), None), P(("group", "block")))
    return jax.shard_map(
        per_device, mesh=mesh, in_specs=placed, out_specs=P(("group", "block")), check_vma=False
    )
```

profile of v0, /device:TPU:1, one launch (start us, length us, event | category | flops | bytes accessed | tf_op | source)
XLA Modules:
  0.0 245.2 jit_solution(18316527973471679262)
XLA Ops:
  6.5 0.8 fusion.4
  7.4 1.1 reduce-window.6
  8.5 0.2 slice_reduce_fusion
  8.8 0.8 fusion.3
  9.5 0.7 compare_select_fusion
  10.2 1.8 multiply_reduce_fusion
  12.0 3.9 %scatter_custom_fusion.1 = bf16[768,1024]{1,0:T(8,128)(2,1)} fusion(s32[512]{0:T(512)S(1)} %bitcast.29, f32[512,1024]{1,0:T(8,128)S(1)} %copy-done, f32[512]{0:T(512)S(1)} %add_rsqrt_fusion, bf16[]{:T(256)} %constant.13.clone.1), kind=kCustom, calls=%fused_computation.6 | custom fusion | flops 1048576 | bytes 3672066 | tf_op jit(solution)/shard_map/scatter | solution.py:18
  15.9 27.7 %all_to_all.33 = bf16[8,96,1024]{2,1,0:T(8,128)(2,1)} all-to-all(bf16[8,96,1024]{2,1,0:T(8,128)(2,1)} %bitcast.22), channel_id=1, replica_groups=mesh['group'=8,'block'=16] {'group'}, dimensions={0} | all-to-all | bytes 3145728 | tf_op jit(solution)/shard_map/all_to_all | solution.py:21
  43.7 2.6 %scatter_custom_fusion = s32[768]{0:T(1024)S(1)} fusion(s32[512]{0:T(512)S(1)} %bitcast.30, s32[512]{0:T(512)} %param.5, s32[]{:T(128)} %constant.9.clone.1), kind=kCustom, calls=%fused_computation.20 | custom fusion | bytes 3584 | tf_op jit(solution)/shard_map/scatter | solution.py:19
  46.3 8.0 %all_to_all.34 = s32[8,96,1]{1,2,0:T(1,128)S(1)} all-to-all(s32[8,96,1]{1,2,0:T(1,128)S(1)} %bitcast.28), channel_id=1, replica_groups=mesh['group'=8,'block'=16] {'group'}, dimensions={0} | all-to-all | bytes 6144 | tf_op jit(solution)/shard_map/all_to_all | solution.py:22
  54.3 0.5 broadcast.70
  54.8 0.7 reduce.10
  55.5 0.1 reshape.73
  55.6 0.1 all_to_all.24
  55.6 20.8 %all-gather = s32[16,1,768]{2,1,0:T(1,128)S(1)} all-gather(s32[1,1,768]{2,1,0:T(1,128)S(1)} %reshape.73), channel_id=1, replica_groups=mesh['group'=8,'block'=16] {'block'}, dimensions={0}, use_global_device_ids=true | all-gather | bytes 52224 | tf_op jit(solution)/shard_map/all_gather | solution.py:25
  76.4 121.4 %all-gather.3.cloned.1.call-done = bf16[12288,1024]{1,0:T(8,128)(2,1)} async-done(((bf16[768,1024]{1,0:T(8,128)(2,1)}), bf16[12288,1024]{1,0:T(8,128)(2,1)}) %all-gather.3.cloned.1.call-update) | async-done | bytes 25165840 | tf_op jit(solution)/shard_map/all_gather | solution.py:28
  197.8 25.5 %select_reduce_fusion = f32[768]{0:T(1024)S(1)} fusion(bf16[768,1024]{1,0:T(8,128)(2,1)} %bitcast.21, bf16[12288,1024]{1,0:T(8,128)(2,1)} %all-gather.3.cloned.1.call-done, s32[12288]{0:T(1024)S(1)} %bitcast.24, s32[768]{0:T(1024)S(1)} %all_to_all.24, pred[12288]{0:T(1024)(128)(4,1)S(1)} %broadcast_compare_fusion), kind=kOutput, calls=%fused_computation.3 | convolution fusion | flops 19365101568 | bytes 26806272 | tf_op jit(solution)/shard_map/dot_general | solution.py:26
  223.3 0.7 max_broadcast_in_dim.14
  224.0 5.1 %all-to-all-start.2 = ((f32[8,96,1]{1,2,0:T(1,128)}), f32[8,96,1]{1,2,0:T(1,128)S(1)}, u32[]{:S(2)}, u32[]{:S(2)}) async-start(f32[8,96,1]{1,2,0:T(1,128)} %bitcast.10), calls=%async_computation.2 | async-start | bytes 8192 | tf_op jit(solution)/shard_map/all_to_all | solution.py:33
  229.1 4.6 %all-to-all-done.2 = f32[8,96,1]{1,2,0:T(1,128)S(1)} async-done(((f32[8,96,1]{1,2,0:T(1,128)}), f32[8,96,1]{1,2,0:T(1,128)S(1)}, u32[]{:S(2)}, u32[]{:S(2)}) %all-to-all-start.2) | async-done | bytes 3104 | tf_op jit(solution)/shard_map/all_to_all | solution.py:33
  233.7 0.5 broadcast.71
  234.2 0.7 reduce.11
  234.8 0.1 all_to_all.29
  234.9 3.4 %gather_fusion = f32[512]{0:T(512)} fusion(f32[768]{0:T(1024)S(1)} %all_to_all.29, s32[1024]{0:T(1024)S(1)} %pad_clamp_fusion), kind=kCustom, calls=%fused_computation | custom fusion | bytes 6144 | tf_op jit(solution)/shard_map/gather | solution.py:34
  (11 shorter events, 0.2 us)
Async XLA Ops:
  6.5 5.5 %copy-start = (f32[512,1024]{1,0:T(8,128)S(1)}, f32[512,1024]{1,0:T(8,128)}, u32[]{:S(2)}) copy-start(f32[512,1024]{1,0:T(8,128)} %param.3) | copy-start | bytes 6291460
  6.5 191.3 %all-gather.3.cloned.1.call-start = ((), (), s32[]{:S(2)}) async-start(), calls=%async_computation.3 | async-start | bytes 26738688 | tf_op jit(solution)/shard_map/all_gather | solution.py:28
  224.0 9.7 %all-to-all-start.2 = ((f32[8,96,1]{1,2,0:T(1,128)}), f32[8,96,1]{1,2,0:T(1,128)S(1)}, u32[]{:S(2)}, u32[]{:S(2)}) async-start(f32[8,96,1]{1,2,0:T(1,128)} %bitcast.10), calls=%async_computation.2 | async-start | bytes 8192 | tf_op jit(solution)/shard_map/all_to_all | solution.py:33
Sparse Core Ops, SparseCore 0:
  43.8 153.9 all-gather.2
where the time goes:
time: 246 us; the launch traced here: 245 us
  waiting for transfers between devices  126 us (51%)
  blocking collectives  56.4 us (23%)
  matrix products  25.5 us (10%)
  between operations  13.5 us (5%)
  other arithmetic  10.5 us (4%)
  local copies, waits for them, and re-layouts  8.22 us (3%)
  starting transfers between devices  5.09 us (2%)
    all_gather x1, waiting for transfers between devices, per_device(): lax.all_gather(local_rows, 'block', axis=0, tiled=True)  121 us
    all_to_all x1, blocking collectives, per_device(): lax.all_to_all(send_rows, 'group', split_axis=0, concat_axis=0, tiled=True)  27.7 us
    dot_general x1, matrix products, per_device(): jnp.dot(local_rows, lax.all_gather(local_rows, 'block', axis=0, tiled=Tru...  25.5 us
    all_gather x1, blocking collectives, per_device(): peer_ids = lax.all_gather(local_ids, 'block', axis=0, tiled=True)  20.8 us
    all_to_all x1, blocking collectives, per_device(): lax.all_to_all(send_ids, 'group', split_axis=0, concat_axis=0, tiled=True)  7.96 us
    all_to_all x1, starting transfers between devices, per_device(): lax.all_to_all(running, 'group', split_axis=0, concat_axis=0, tiled=True)  5.09 us
  transfers between devices with their start and end apart: 2, of which 2 were waited for; matrix products, arithmetic and copies ran while one was open for 2% of the time, Pallas kernels for 0%

commit v1 on v0

v1 whole, which is shorter than its diff:
```python
import functools
import jax
import jax.numpy as jnp
from jax import lax
from jax.experimental import pallas as pl
from jax.experimental.pallas import tpu as pltpu
from jax.sharding import PartitionSpec as P

SIDE = 4
ROWS = 512
FEATURES = 1024
GROUPS = 8
CAPACITY = 96
HALF = CAPACITY // 2
EXTRA = 16
FIRST = HALF + EXTRA
PART = GROUPS * HALF
BLOCK = 2 * PART
MIB = 1 << 20
VMEM = pl.BlockSpec(memory_space=pltpu.VMEM)
ANY = pl.BlockSpec(memory_space=pl.ANY)
NT = (((1,), (1,)), ((), ()))


def column_of(row):
    return jnp.transpose(jnp.broadcast_to(row, (128, row.shape[1])))


def spread(row, lanes):
    return jnp.concatenate([column_of(row)] * (lanes // 128), axis=1)


def prepare_kernel(group_ref, emb_ref, label_ref, id_ref, first_ref, second_ref, place_ref):
    values = emb_ref[...]
    scale = lax.rsqrt(jnp.sum(values * values, axis=1, keepdims=True) + 1e-06)
    normed = (values * scale).astype(jnp.bfloat16)
    labels = label_ref[...]
    ids = id_ref[...]
    before = lax.broadcasted_iota(jnp.int32, (ROWS, ROWS), 0) < lax.broadcasted_iota(jnp.int32, (ROWS, ROWS), 1)
    alike = spread(labels, ROWS) == labels
    rank = jnp.sum((before & alike).astype(jnp.int32), axis=0, keepdims=True)
    in_first = rank < HALF
    within = jnp.where(in_first, rank, rank - HALF)
    to_first = jnp.where(in_first, labels * FIRST + rank, -1)
    to_second = jnp.where(in_first, -1, labels * HALF + within)

    def pick(target, count):
        return (lax.broadcasted_iota(jnp.int32, (count, ROWS), 0) == target).astype(jnp.bfloat16)

    def moved(target, count):
        return jnp.dot(pick(target, count), normed, preferred_element_type=jnp.float32).astype(jnp.bfloat16)

    first_ref[...] = moved(to_first, GROUPS * FIRST)
    second_ref[...] = moved(to_second, PART)
    place_ref[...] = jnp.where(in_first, 0, PART) + labels * HALF + within
    kind = lax.broadcasted_iota(jnp.int32, (8, ROWS), 0)
    digits = jnp.where(kind == 0, ids & 255, jnp.where(kind == 1, ids >> 8, jnp.where(kind == 2, 1, 0)))
    digits = jnp.concatenate([jnp.where(labels == c, digits, 0) for c in range(GROUPS)], axis=0)
    lane = jnp.where(in_first, 0, PART) + group_ref[0] * HALF + within
    digits = lax.dot_general(digits.astype(jnp.float32).astype(jnp.bfloat16), pick(lane, FEATURES), NT,
                             preferred_element_type=jnp.float32)
    for c in range(GROUPS):
        start = c * FIRST + HALF
        extra = jnp.concatenate([digits[8 * c:8 * c + 8], jnp.zeros((8, FEATURES), jnp.float32)], axis=0)
        first_ref[start:start + EXTRA, :] = extra.astype(jnp.bfloat16)


def prepare(embeddings, labels, row_ids, group):
    return pl.pallas_call(
        prepare_kernel,
        out_shape=(
            jax.ShapeDtypeStruct((GROUPS * FIRST, FEATURES), jnp.bfloat16),
            jax.ShapeDtypeStruct((PART, FEATURES), jnp.bfloat16),
            jax.ShapeDtypeStruct((1, ROWS), jnp.int32),
        ),
        in_specs=[pl.BlockSpec(memory_space=pltpu.SMEM)] + [VMEM] * 3,
        out_specs=(VMEM,) * 3,
        compiler_params=pltpu.CompilerParams(vmem_limit_bytes=32 * MIB),
        name="prepare",
    )(group, embeddings, labels, row_ids)


def gather_kernel(first_ref, out_ref):
    extra = jnp.zeros((EXTRA, FEATURES), jnp.float32)
    for s in range(GROUPS):
        out_ref[s * HALF:(s + 1) * HALF, :] = first_ref[s * FIRST:s * FIRST + HALF, :]
        extra = extra + first_ref[s * FIRST + HALF:(s + 1) * FIRST, :].astype(jnp.float32)
    out_ref[PART:PART + EXTRA, :] = extra.astype(jnp.bfloat16)


def gather_first(first):
    return pl.pallas_call(
        gather_kernel,
        out_shape=jax.ShapeDtypeStruct((PART + EXTRA, FEATURES), jnp.bfloat16),
        in_specs=[VMEM], out_specs=VMEM,
        compiler_params=pltpu.CompilerParams(vmem_limit_bytes=16 * MIB),
        name="gather_first",
    )(first)


def column_keys(extra):
    digits = extra[:, 0:BLOCK].astype(jnp.float32)
    return digits[0:1] + digits[1:2] * 256.0 + (1.0 - digits[2:3]) * 131072.0


def row_keys(extra):
    digit = lax.broadcasted_iota(jnp.int32, (EXTRA, 128), 0)
    weight = jnp.where(digit == 0, 1.0, jnp.where(digit == 1, 256.0, 0.0)).astype(jnp.bfloat16)
    return lax.dot_general(extra[:, 0:BLOCK], weight, (((0,), (0,)), ((), ())), preferred_element_type=jnp.float32)


def compare_kernel(products, names, *refs):
    count = len(names)
    sources = refs[:2 * count]
    before_ref, out_ref, held, extra, best, keys, sems = refs[2 * count:]
    copies = []
    for n in range(count):
        first, second = sources[2 * n], sources[2 * n + 1]
        copies.append((
            pltpu.make_async_copy(first.at[0:PART], held.at[n, 0:PART], sems.at[3 * n]),
            pltpu.make_async_copy(first.at[PART:PART + EXTRA], extra.at[n], sems.at[3 * n + 1]),
            pltpu.make_async_copy(second, held.at[n, PART:BLOCK], sems.at[3 * n + 2]),
        ))
        for copy in copies[-1]:
            copy.start()
    for group in copies:
        for copy in group:
            copy.wait()
    best[...] = jnp.full(best.shape, -1.0, jnp.float32)
    for n in range(count):
        keys[n] = row_keys(extra[n])

    def product(rows, columns):
        theirs = column_keys(extra[columns])
        for r in range(0, BLOCK, PART):
            scores = lax.dot_general(held[rows, r:r + PART, :], held[columns], NT, preferred_element_type=jnp.float32)
            own = jnp.concatenate([keys[rows, r:r + PART, :]] * (BLOCK // 128), axis=1)
            earlier = jnp.where(theirs < own, scores, -1.0)
            earlier = functools.reduce(jnp.maximum, [earlier[:, c:c + 128] for c in range(0, BLOCK, 128)])
            best[rows, r:r + PART, :] = jnp.maximum(best[rows, r:r + PART, :], earlier)

    for rows, columns in products:
        lax.fori_loop(0, len(rows) * len(columns), functools.partial(pair_step, product, rows, columns), 0)
    used = sorted({r for rows, _ in products for r in rows})
    out_ref[...] = before_ref[...]
    for r in used:
        found = jnp.max(jnp.transpose(best[r]), axis=0, keepdims=True)
        place = LINE.index(names[r])
        out_ref[place:place + 1, :] = jnp.maximum(out_ref[place:place + 1, :], found)


def pair_step(product, rows, columns, step, carry):
    product(rows[0] + lax.div(step, len(columns)), columns[0] + lax.rem(step, len(columns)))
    return carry


LINE = ("own", "xp", "xm", "xo")


def compare(names, products, blocks, best, name):
    count = len(names)
    operands = [part for n in names for part in blocks[n]]
    units = sum(len(r) * len(c) for r, c in products)
    return pl.pallas_call(
        functools.partial(compare_kernel, products, names),
        out_shape=jax.ShapeDtypeStruct((8, BLOCK), jnp.float32),
        in_specs=[ANY] * (2 * count) + [VMEM],
        out_specs=VMEM,
        scratch_shapes=[
            pltpu.VMEM((count, BLOCK, FEATURES), jnp.bfloat16),
            pltpu.VMEM((count, EXTRA, FEATURES), jnp.bfloat16),
            pltpu.VMEM((count, BLOCK, 128), jnp.float32),
            pltpu.VMEM((count, BLOCK, 128), jnp.float32),
            pltpu.SemaphoreType.DMA((3 * count,)),
        ],
        compiler_params=pltpu.CompilerParams(vmem_limit_bytes=40 * MIB),
        cost_estimate=pl.CostEstimate(flops=2 * units * BLOCK * BLOCK * FEATURES,
                                      bytes_accessed=count * 2 * BLOCK * FEATURES, transcendentals=0),
        name=name,
    )(*operands, best)


def finish_kernel(place_ref, value_ref, out_ref):
    here = lax.broadcasted_iota(jnp.int32, (BLOCK, ROWS), 0) == place_ref[...]
    out_ref[...] = jnp.max(jnp.where(here, spread(value_ref[...], ROWS), -2.0), axis=0, keepdims=True)


def move(value, dx, dy):
    pairs = [(y * SIDE + x, (y + dy) % SIDE * SIDE + (x + dx) % SIDE) for y in range(SIDE) for x in range(SIDE)]
    return lax.ppermute(value, "block", pairs)


def exchange(value):
    return lax.all_to_all(value, "group", split_axis=0, concat_axis=0, tiled=True)


def per_device(embeddings, labels, row_ids):
    group = lax.axis_index("group").astype(jnp.int32).reshape(1)
    first, second, place = prepare(embeddings, labels.reshape(1, ROWS), row_ids.reshape(1, ROWS), group)
    first = gather_first(exchange(first))
    second, first = lax.optimization_barrier((second, first))
    second = exchange(second)
    xp, xm, yp, ym = move(first, -1, 0), move(first, 1, 0), move(first, 0, -1), move(first, 0, 1)
    second, xp, xm, yp, ym = lax.optimization_barrier((second, xp, xm, yp, ym))
    xp2, xm2, yp2, ym2 = move(second, -1, 0), move(second, 1, 0), move(second, 0, -1), move(second, 0, 1)
    xo, yo = move(xp, -1, 0), move(yp, 0, -1)
    xo2, yo2 = move(xm2, 1, 0), move(ym2, 0, 1)
    blocks = dict(own=(first, second), xp=(xp, xp2), xm=(xm, xm2), yp=(yp, yp2), ym=(ym, ym2),
                  xo=(xo, xo2), yo=(yo, yo2))
    best = jnp.full((8, BLOCK), -1.0, jnp.float32)
    best = compare(("xp", "xm", "own", "yp", "ym"), (((0, 1, 2), (2, 3, 4)),), blocks, best, "compare_near")
    best = compare(("xo", "xp", "xm", "own", "yp", "ym", "yo"), (((0,), (3, 4, 5)), ((0, 1, 2, 3), (6,))),
                   blocks, best, "compare_far")
    own = best[0:1]
    for row, dx in ((1, 1), (2, -1), (3, 2)):
        own = jnp.maximum(own, move(best[row:row + 1], dx, 0))
    back = lax.all_to_all(own.reshape(2, GROUPS, HALF), "group", split_axis=1, concat_axis=1, tiled=True)
    out = pl.pallas_call(
        finish_kernel, out_shape=jax.ShapeDtypeStruct((1, ROWS), jnp.float32), name="finish",
    )(place, back.reshape(1, BLOCK))
    return out.reshape(ROWS)


def solution(mesh):
    placed = (P(("group", "block"), None), P(("group", "block"), None), P(("group", "block")))
    return jax.shard_map(
        per_device, mesh=mesh, in_specs=placed, out_specs=P(("group", "block")), check_vma=False
    )
```

time: 246 us -> 121 us (0.49)
  waiting for transfers between devices: 126 us -> 16.3 us
  Pallas kernels: 0 us -> 30.4 us
  matrix products: 25.5 us -> 0 us
  between operations: 13.5 us -> 0.08 us
  starting transfers between devices: 5.09 us -> 18.4 us
  other arithmetic: 10.5 us -> 0.02 us
  local copies, waits for them, and re-layouts: 8.22 us -> 3.73 us
  blocking collectives: 56.4 us -> 52 us
    all_gather x1 -> x0, waiting for transfers between devices: 121 us -> none  [per_device(): lax.all_gather(local_rows, 'block', axis=0, tiled=True)]
    pallas_call x0 -> x5, Pallas kernels: none -> 30.4 us  [the longest x2 27 us: compare(): pl.pallas_call(functools.partial(compare_kernel, products, names), out_sh...]
    dot_general x1 -> x0, matrix products: 25.5 us -> none  [per_device(): jnp.dot(local_rows, lax.all_gather(local_rows, 'block', axis=0, tiled=Tru...]
    all_gather x1 -> x0, blocking collectives: 20.8 us -> none  [per_device(): peer_ids = lax.all_gather(local_ids, 'block', axis=0, tiled=True)]
    ppermute x0 -> x15, starting transfers between devices: none -> 18.4 us  [move(): return lax.ppermute(value, 'block', pairs)]
    all_to_all x2 -> x3, blocking collectives: 35.6 us -> 52 us  [the longest x2 38.3 us: exchange(): lax.all_to_all(value, 'group', split_axis=0, concat_axis=0, tiled=True)]
    ppermute x0 -> x15, waiting for transfers between devices: none -> 16.3 us  [move(): return lax.ppermute(value, 'block', pairs)]
    all_to_all x1 -> x0, starting transfers between devices: 5.09 us -> none  [per_device(): lax.all_to_all(running, 'group', split_axis=0, concat_axis=0, tiled=True)]
  transfers between devices with their start and end apart: 2 -> 15, of which waited for: 2 -> 6; matrix products, arithmetic and copies ran while one was open for 2% -> 0% of each run, Pallas kernels for 0% -> 12%
where the time goes in v1:
time: 121 us
  blocking collectives  52 us (43%)
  Pallas kernels  30.4 us (25%)
  starting transfers between devices  18.4 us (15%)
  waiting for transfers between devices  16.3 us (13%)
  local copies, waits for them, and re-layouts  3.73 us (3%)
    all_to_all x2, blocking collectives, exchange(): lax.all_to_all(value, 'group', split_axis=0, concat_axis=0, tiled=True)  38.3 us
    pallas_call x2, Pallas kernels, compare(): pl.pallas_call(functools.partial(compare_kernel, products, names), out_sh...  27 us
    ppermute x15, starting transfers between devices, move(): return lax.ppermute(value, 'block', pairs)  18.4 us
    ppermute x15, waiting for transfers between devices, move(): return lax.ppermute(value, 'block', pairs)  16.3 us
    all_to_all x1, blocking collectives, per_device(): lax.all_to_all(own.reshape(2, GROUPS, HALF), 'group', split_axis=1, conca...  13.7 us
    unnamed x8, local copies, waits for them, and re-layouts  2.96 us
  transfers between devices with their start and end apart: 15, of which 6 were waited for; matrix products, arithmetic and copies ran while one was open for 0% of the time, Pallas kernels for 12%

profile of v1, /device:TPU:1, one launch (start us, length us, event | category | flops | bytes accessed | tf_op | source)
XLA Modules:
  0.0 120.9 jit_solution(13040960982080041187)
XLA Ops:
  0.0 1.6 %copy-done = f32[512,1024]{1,0:T(8,128)S(1)} copy-done((f32[512,1024]{1,0:T(8,128)S(1)}, f32[512,1024]{1,0:T(8,128)}, u32[]{:S(2)}) %copy-start) | copy-done | bytes 2097176
  1.6 0.7 copy-done.1
  3.0 1.7 %prepare.1 = (bf16[512,1024]{1,0:T(8,128)(2,1)S(1)}, bf16[384,1024]{1,0:T(8,128)(2,1)S(1)}, s32[1,512]{1,0:T(1,128)S(1)}) custom-call(s32[1]{0:T(128)} %bitcast.group_ref, f32[512,1024]{1,0:T(8,128)S(1)} %copy-done, s32[1,512]{1,0:T(1,128)S(1)} %bitcast.17, s32[1,512]{1,0:T(1,128)S(1)} %bitcast.18), custom_call_target="tpu_custom_call" | custom-call | tf_op jit(solution)/shard_map/prepare/pallas_call | solution.py:69
  4.6 21.7 %all_to_all.28 = bf16[8,64,1024]{2,1,0:T(8,128)(2,1)S(1)} all-to-all(bf16[8,64,1024]{2,1,0:T(8,128)(2,1)S(1)} %bitcast.9), channel_id=1, replica_groups=mesh['group'=8,'block'=16] {'group'}, dimensions={0} | all-to-all | bytes 2097152 | tf_op jit(solution)/shard_map/all_to_all | solution.py:194
  26.4 1.4 %collective-permute-start.3 = (bf16[400,1024]{1,0:T(8,128)(2,1)S(1)}, bf16[400,1024]{1,0:T(8,128)(2,1)S(1)}, u32[]{:S(2)}, u32[]{:S(2)}) collective-permute-start(bf16[400,1024]{1,0:T(8,128)(2,1)S(1)} %gather_first.1.refs_4_.refs_6_), channel_id=1, source_target_pairs={{0,4},{1,5},{2,6},{3,7},{4,8},{5,9},{6,10},{7,11},{8,12},{9,13},{1... | collective-permute-start | bytes 2457608 | tf_op jit(solution)/shard_map/ppermute | solution.py:190
  27.8 1.5 %collective-permute-start.2 = (bf16[400,1024]{1,0:T(8,128)(2,1)S(1)}, bf16[400,1024]{1,0:T(8,128)(2,1)S(1)}, u32[]{:S(2)}, u32[]{:S(2)}) collective-permute-start(bf16[400,1024]{1,0:T(8,128)(2,1)S(1)} %gather_first.1.refs_4_.refs_6_), channel_id=1, source_target_pairs={{0,12},{1,13},{2,14},{3,15},{4,0},{5,1},{6,2},{7,3},{8,4},{9,5},{1... | collective-permute-start | bytes 2457608 | tf_op jit(solution)/shard_map/ppermute | solution.py:190
  29.3 1.2 %collective-permute-start.1 = (bf16[400,1024]{1,0:T(8,128)(2,1)S(1)}, bf16[400,1024]{1,0:T(8,128)(2,1)S(1)}, u32[]{:S(2)}, u32[]{:S(2)}) collective-permute-start(bf16[400,1024]{1,0:T(8,128)(2,1)S(1)} %gather_first.1.refs_4_.refs_6_), channel_id=1, source_target_pairs={{0,1},{1,2},{2,3},{3,0},{4,5},{5,6},{6,7},{7,4},{8,9},{9,10},{10,1... | collective-permute-start | bytes 2457608 | tf_op jit(solution)/shard_map/ppermute | solution.py:190
  30.5 1.5 %collective-permute-start = (bf16[400,1024]{1,0:T(8,128)(2,1)S(1)}, bf16[400,1024]{1,0:T(8,128)(2,1)S(1)}, u32[]{:S(2)}, u32[]{:S(2)}) collective-permute-start(bf16[400,1024]{1,0:T(8,128)(2,1)S(1)} %gather_first.1.refs_4_.refs_6_), channel_id=1, source_target_pairs={{0,3},{1,0},{2,1},{3,2},{4,7},{5,4},{6,5},{7,6},{8,11},{9,8},{10,9... | collective-permute-start | bytes 2457608 | tf_op jit(solution)/shard_map/ppermute | solution.py:190
  32.0 16.6 %all_to_all.29 = bf16[8,48,1024]{2,1,0:T(8,128)(2,1)S(1)} all-to-all(bf16[8,48,1024]{2,1,0:T(8,128)(2,1)S(1)} %bitcast.16), channel_id=1, replica_groups=mesh['group'=8,'block'=16] {'group'}, dimensions={0} | all-to-all | bytes 1572864 | tf_op jit(solution)/shard_map/all_to_all | solution.py:194
  48.8 2.7 %collective-permute-start.8 = (bf16[384,1024]{1,0:T(8,128)(2,1)S(1)}, bf16[384,1024]{1,0:T(8,128)(2,1)S(1)}, u32[]{:S(2)}, u32[]{:S(2)}) collective-permute-start(bf16[384,1024]{1,0:T(8,128)(2,1)S(1)} %bitcast.11), channel_id=1, source_target_pairs={{0,12},{1,13},{2,14},{3,15},{4,0},{5,1},{6,2},{7,3},{8,4},{9,5},{1... | collective-permute-start | bytes 2359304 | tf_op jit(solution)/shard_map/ppermute | solution.py:190
  51.4 0.9 collective-permute-start.5
  52.4 1.8 %collective-permute-start.7 = (bf16[384,1024]{1,0:T(8,128)(2,1)S(1)}, bf16[384,1024]{1,0:T(8,128)(2,1)S(1)}, u32[]{:S(2)}, u32[]{:S(2)}) collective-permute-start(bf16[384,1024]{1,0:T(8,128)(2,1)S(1)} %bitcast.13), channel_id=1, source_target_pairs={{0,3},{1,0},{2,1},{3,2},{4,7},{5,4},{6,5},{7,6},{8,11},{9,8},{10,9... | collective-permute-start | bytes 2359304 | tf_op jit(solution)/shard_map/ppermute | solution.py:190
  54.1 1.2 collective-permute-start.4
  55.3 11.3 %collective-permute-done.9.refs_9_.refs_11_ = bf16[384,1024]{1,0:T(8,128)(2,1)S(1)} collective-permute-done((bf16[384,1024]{1,0:T(8,128)(2,1)S(1)}, bf16[384,1024]{1,0:T(8,128)(2,1)S(1)}, u32[]{:S(2)}, u32[]{:S(2)}) %collective-permute-start.9) | collective-permute-done | bytes 786464 | tf_op jit(solution)/shard_map/ppermute | solution.py:190
  66.9 1.2 collective-permute-start.11
  68.8 14.7 %compare_near.1.refs_14_ = f32[8,768]{1,0:T(8,128)S(1)} custom-call(bf16[400,1024]{1,0:T(8,128)(2,1)S(1)} %collective-permute-done.refs_0_.refs_2_, bf16[384,1024]{1,0:T(8,128)(2,1)S(1)} %collective-permute-done.7.refs_1_.refs_3_, bf16[400,1024]{1,0:T(8,128)(2,1)S(1)} %collective-permute-done.1.refs_2_.refs_4_, ...), custom_call_target="tpu_custom_call" | custom-call | flops 10871635968 | bytes 7864320 | tf_op jit(solution)/shard_map/compare_near/pallas_call | solution.py:164
  83.4 2.0 %collective-permute-done.4.refs_0_ = bf16[400,1024]{1,0:T(8,128)(2,1)S(1)} collective-permute-done((bf16[400,1024]{1,0:T(8,128)(2,1)S(1)}, bf16[400,1024]{1,0:T(8,128)(2,1)S(1)}, u32[]{:S(2)}, u32[]{:S(2)}) %collective-permute-start.4) | collective-permute-done | bytes 819232 | tf_op jit(solution)/shard_map/ppermute | solution.py:190
  85.5 12.4 %compare_far.1 = f32[8,768]{1,0:T(8,128)S(1)} custom-call(bf16[400,1024]{1,0:T(8,128)(2,1)S(1)} %collective-permute-done.4.refs_0_, bf16[384,1024]{1,0:T(8,128)(2,1)S(1)} %collective-permute-done.6.refs_1_, bf16[400,1024]{1,0:T(8,128)(2,1)S(1)} %collective-permute-done.refs_0_.refs_2_, bf16[384,1024]{1,0:T(8,128)(2,1)S(1)} %collective-permute-done.7.refs_1_.refs_3_, ...), custom_call_target="tpu_custom_call" | custom-call | flops 8455716864 | bytes 11010048 | tf_op jit(solution)/shard_map/compare_far/pallas_call | solution.py:164
  97.9 1.0 collective-permute-start.12
  98.9 3.5 %collective-permute-start.14 = (f32[1,768]{1,0:T(1,128)S(1)}, f32[1,768]{1,0:T(1,128)S(1)}, u32[]{:S(2)}, u32[]{:S(2)}) collective-permute-start(f32[1,768]{1,0:T(1,128)S(1)} %get-tuple-element.26), channel_id=1, source_target_pairs={{0,2},{1,3},{2,0},{3,1},{4,6},{5,7},{6,4},{7,5},{8,10},{9,11},{10,... | collective-permute-start | bytes 9224 | tf_op jit(solution)/shard_map/ppermute | solution.py:190
  102.7 0.7 collective-permute-done.14
  103.4 1.4 %collective-permute-done.13 = f32[1,768]{1,0:T(1,128)S(1)} collective-permute-done((f32[1,768]{1,0:T(1,128)S(1)}, f32[1,768]{1,0:T(1,128)S(1)}, u32[]{:S(2)}, u32[]{:S(2)}) %collective-permute-start.13) | collective-permute-done | bytes 3104 | tf_op jit(solution)/shard_map/ppermute | solution.py:190
  104.9 13.7 %all_to_all.30 = f32[2,8,48]{2,0,1:T(2,128)S(1)} all-to-all(f32[2,8,48]{2,0,1:T(2,128)S(1)} %copy.4), channel_id=1, replica_groups=mesh['group'=8,'block'=16] {'group'}, dimensions={1} | all-to-all | bytes 6144 | tf_op jit(solution)/shard_map/all_to_all | solution.py:217
  119.3 1.6 %finish.1 = f32[1,512]{1,0:T(1,128)} custom-call(s32[1,512]{1,0:T(1,128)} %copy-done.3, f32[1,768]{1,0:T(1,128)} %reshape.26.value_ref), custom_call_target="tpu_custom_call" | custom-call | tf_op jit(solution)/shard_map/finish/pallas_call | solution.py:218
  (29 shorter events, 3.0 us)
Async XLA Ops:
  0.0 1.6 %copy-start = (f32[512,1024]{1,0:T(8,128)S(1)}, f32[512,1024]{1,0:T(8,128)}, u32[]{:S(2)}) copy-start(f32[512,1024]{1,0:T(8,128)} %emb_ref.1) | copy-start | bytes 6291460
  1.6 0.7 copy-start.1
  2.3 0.7 copy-start.2
  4.6 44.0 %copy-start.3 = (s32[1,512]{1,0:T(1,128)}, s32[1,512]{1,0:T(1,128)S(1)}, u32[]{:S(2)}) copy-start(s32[1,512]{1,0:T(1,128)S(1)} %get-tuple-element.15.place_ref) | copy-start | bytes 6148
  26.4 22.2 %collective-permute-start.3 = (bf16[400,1024]{1,0:T(8,128)(2,1)S(1)}, bf16[400,1024]{1,0:T(8,128)(2,1)S(1)}, u32[]{:S(2)}, u32[]{:S(2)}) collective-permute-start(bf16[400,1024]{1,0:T(8,128)(2,1)S(1)} %gather_first.1.refs_4_.refs_6_), channel_id=1, source_target_pairs={{0,4},{1,5},{2,6},{3,7},{4,8},{5,9},{6,10},{7,11},{8,12},{9,13},{1... | collective-permute-start | bytes 2457608 | tf_op jit(solution)/shard_map/ppermute | solution.py:190
  27.8 20.8 %collective-permute-start.2 = (bf16[400,1024]{1,0:T(8,128)(2,1)S(1)}, bf16[400,1024]{1,0:T(8,128)(2,1)S(1)}, u32[]{:S(2)}, u32[]{:S(2)}) collective-permute-start(bf16[400,1024]{1,0:T(8,128)(2,1)S(1)} %gather_first.1.refs_4_.refs_6_), channel_id=1, source_target_pairs={{0,12},{1,13},{2,14},{3,15},{4,0},{5,1},{6,2},{7,3},{8,4},{9,5},{1... | collective-permute-start | bytes 2457608 | tf_op jit(solution)/shard_map/ppermute | solution.py:190
  29.3 19.5 %collective-permute-start.1 = (bf16[400,1024]{1,0:T(8,128)(2,1)S(1)}, bf16[400,1024]{1,0:T(8,128)(2,1)S(1)}, u32[]{:S(2)}, u32[]{:S(2)}) collective-permute-start(bf16[400,1024]{1,0:T(8,128)(2,1)S(1)} %gather_first.1.refs_4_.refs_6_), channel_id=1, source_target_pairs={{0,1},{1,2},{2,3},{3,0},{4,5},{5,6},{6,7},{7,4},{8,9},{9,10},{10,1... | collective-permute-start | bytes 2457608 | tf_op jit(solution)/shard_map/ppermute | solution.py:190
  30.5 18.3 %collective-permute-start = (bf16[400,1024]{1,0:T(8,128)(2,1)S(1)}, bf16[400,1024]{1,0:T(8,128)(2,1)S(1)}, u32[]{:S(2)}, u32[]{:S(2)}) collective-permute-start(bf16[400,1024]{1,0:T(8,128)(2,1)S(1)} %gather_first.1.refs_4_.refs_6_), channel_id=1, source_target_pairs={{0,3},{1,0},{2,1},{3,2},{4,7},{5,4},{6,5},{7,6},{8,11},{9,8},{10,9... | collective-permute-start | bytes 2457608 | tf_op jit(solution)/shard_map/ppermute | solution.py:190
  48.8 17.9 %collective-permute-start.9 = (bf16[384,1024]{1,0:T(8,128)(2,1)S(1)}, bf16[384,1024]{1,0:T(8,128)(2,1)S(1)}, u32[]{:S(2)}, u32[]{:S(2)}) collective-permute-start(bf16[384,1024]{1,0:T(8,128)(2,1)S(1)} %bitcast.10), channel_id=1, source_target_pairs={{0,4},{1,5},{2,6},{3,7},{4,8},{5,9},{6,10},{7,11},{8,12},{9,13},{1... | collective-permute-start | bytes 2359304 | tf_op jit(solution)/shard_map/ppermute | solution.py:190
  48.8 18.1 %collective-permute-start.8 = (bf16[384,1024]{1,0:T(8,128)(2,1)S(1)}, bf16[384,1024]{1,0:T(8,128)(2,1)S(1)}, u32[]{:S(2)}, u32[]{:S(2)}) collective-permute-start(bf16[384,1024]{1,0:T(8,128)(2,1)S(1)} %bitcast.11), channel_id=1, source_target_pairs={{0,12},{1,13},{2,14},{3,15},{4,0},{5,1},{6,2},{7,3},{8,4},{9,5},{1... | collective-permute-start | bytes 2359304 | tf_op jit(solution)/shard_map/ppermute | solution.py:190
  51.4 17.3 %collective-permute-start.5 = (bf16[384,1024]{1,0:T(8,128)(2,1)S(1)}, bf16[384,1024]{1,0:T(8,128)(2,1)S(1)}, u32[]{:S(2)}, u32[]{:S(2)}) collective-permute-start(bf16[384,1024]{1,0:T(8,128)(2,1)S(1)} %bitcast.12), channel_id=1, source_target_pairs={{0,1},{1,2},{2,3},{3,0},{4,5},{5,6},{6,7},{7,4},{8,9},{9,10},{10,1... | collective-permute-start | bytes 2359304 | tf_op jit(solution)/shard_map/ppermute | solution.py:190
  52.4 16.4 %collective-permute-start.7 = (bf16[384,1024]{1,0:T(8,128)(2,1)S(1)}, bf16[384,1024]{1,0:T(8,128)(2,1)S(1)}, u32[]{:S(2)}, u32[]{:S(2)}) collective-permute-start(bf16[384,1024]{1,0:T(8,128)(2,1)S(1)} %bitcast.13), channel_id=1, source_target_pairs={{0,3},{1,0},{2,1},{3,2},{4,7},{5,4},{6,5},{7,6},{8,11},{9,8},{10,9... | collective-permute-start | bytes 2359304 | tf_op jit(solution)/shard_map/ppermute | solution.py:190
  54.1 31.3 %collective-permute-start.4 = (bf16[400,1024]{1,0:T(8,128)(2,1)S(1)}, bf16[400,1024]{1,0:T(8,128)(2,1)S(1)}, u32[]{:S(2)}, u32[]{:S(2)}) collective-permute-start(bf16[400,1024]{1,0:T(8,128)(2,1)S(1)} %collective-permute-done.refs_0_.refs_2_), channel_id=1, source_target_pairs={{0,3},{1,0},{2,1},{3,2},{4,7},{5,4},{6,5},{7,6},{8,11},{9,8},{10,9... | collective-permute-start | bytes 2457608 | tf_op jit(solution)/shard_map/ppermute | solution.py:190
  66.6 18.8 %collective-permute-start.10 = (bf16[400,1024]{1,0:T(8,128)(2,1)S(1)}, bf16[400,1024]{1,0:T(8,128)(2,1)S(1)}, u32[]{:S(2)}, u32[]{:S(2)}) collective-permute-start(bf16[400,1024]{1,0:T(8,128)(2,1)S(1)} %collective-permute-done.2.refs_6_.refs_8_), channel_id=1, source_target_pairs={{0,12},{1,13},{2,14},{3,15},{4,0},{5,1},{6,2},{7,3},{8,4},{9,5},{1... | collective-permute-start | bytes 2457608 | tf_op jit(solution)/shard_map/ppermute | solution.py:190
  66.9 18.5 %collective-permute-start.11 = (bf16[384,1024]{1,0:T(8,128)(2,1)S(1)}, bf16[384,1024]{1,0:T(8,128)(2,1)S(1)}, u32[]{:S(2)}, u32[]{:S(2)}) collective-permute-start(bf16[384,1024]{1,0:T(8,128)(2,1)S(1)} %collective-permute-done.9.refs_9_.refs_11_), channel_id=1, source_target_pairs={{0,4},{1,5},{2,6},{3,7},{4,8},{5,9},{6,10},{7,11},{8,12},{9,13},{1... | collective-permute-start | bytes 2359304 | tf_op jit(solution)/shard_map/ppermute | solution.py:190
  68.7 16.7 %collective-permute-start.6 = (bf16[384,1024]{1,0:T(8,128)(2,1)S(1)}, bf16[384,1024]{1,0:T(8,128)(2,1)S(1)}, u32[]{:S(2)}, u32[]{:S(2)}) collective-permute-start(bf16[384,1024]{1,0:T(8,128)(2,1)S(1)} %collective-permute-done.5.refs_3_.refs_5_), channel_id=1, source_target_pairs={{0,1},{1,2},{2,3},{3,0},{4,5},{5,6},{6,7},{7,4},{8,9},{9,10},{10,1... | collective-permute-start | bytes 2359304 | tf_op jit(solution)/shard_map/ppermute | solution.py:190
  97.9 4.8 %collective-permute-start.12 = (f32[1,768]{1,0:T(1,128)S(1)}, f32[1,768]{1,0:T(1,128)S(1)}, u32[]{:S(2)}, u32[]{:S(2)}) collective-permute-start(f32[1,768]{1,0:T(1,128)S(1)} %get-tuple-element.25), channel_id=1, source_target_pairs={{0,1},{1,2},{2,3},{3,0},{4,5},{5,6},{6,7},{7,4},{8,9},{9,10},{10,1... | collective-permute-start | bytes 9224 | tf_op jit(solution)/shard_map/ppermute | solution.py:190
  98.9 4.5 %collective-permute-start.14 = (f32[1,768]{1,0:T(1,128)S(1)}, f32[1,768]{1,0:T(1,128)S(1)}, u32[]{:S(2)}, u32[]{:S(2)}) collective-permute-start(f32[1,768]{1,0:T(1,128)S(1)} %get-tuple-element.26), channel_id=1, source_target_pairs={{0,2},{1,3},{2,0},{3,1},{4,6},{5,7},{6,4},{7,5},{8,10},{9,11},{10,... | collective-permute-start | bytes 9224 | tf_op jit(solution)/shard_map/ppermute | solution.py:190
  102.4 2.4 %collective-permute-start.13 = (f32[1,768]{1,0:T(1,128)S(1)}, f32[1,768]{1,0:T(1,128)S(1)}, u32[]{:S(2)}, u32[]{:S(2)}) collective-permute-start(f32[1,768]{1,0:T(1,128)S(1)} %get-tuple-element.27), channel_id=1, source_target_pairs={{0,3},{1,0},{2,1},{3,2},{4,7},{5,4},{6,5},{7,6},{8,11},{9,8},{10,9... | collective-permute-start | bytes 9224 | tf_op jit(solution)/shard_map/ppermute | solution.py:190
